TPU v7x, 512 devices: a whole 4x8x8 slice. The times are simulated.
512 devices in a mesh: seq: 64 (over x, y, core), mp: 8 (over z).
Axes of the slice: x: 4, y: 8, z: 8, core: 2. Of those that a mesh axis runs over, the one named last changes fastest.
Arguments:
- token_ids: int32 [96, 2], replicated, may hold values from 0 to 25599
- prompt_lengths: int32 [6], replicated, may hold values from 1024 to 8192, as said below
- tail_lengths: int32 [96], replicated, may hold values from 32 to 256, as said below
- prompt_of: int32 [96], replicated, may hold values from 0 to 5, as said below
- page_table: int32 [96, 2], replicated, may hold values from 0 to 191, as said below
- prompt_keys: bfloat16 [49152, 6144], P('seq', 'mp'), may hold values from -240 to 240
- prompt_values: bfloat16 [49152, 6144], P('seq', 'mp'), may hold values from -12 to 12
- tail_keys: bfloat16 [24576, 6144], P('seq', 'mp'), may hold values from -240 to 240
- tail_values: bfloat16 [24576, 6144], P('seq', 'mp'), may hold values from -12 to 12
- norm_gain: bfloat16 [2, 7168], P(None, 'seq'), may hold values from 0.5 to 1.5
- norm_bias: bfloat16 [2, 7168], P(None, 'seq'), may hold values from -2 to 2
- qkv_weight: bfloat16 [7168, 3, 6144], P('seq', None, 'mp'), may hold values from -0.0625 to 0.0625
- qkv_bias: bfloat16 [3, 6144], P(None, 'mp'), may hold values from -2 to 2
- out_weight: bfloat16 [6144, 7168], P('mp', 'seq'), may hold values from -0.078125 to 0.078125
- out_bias: bfloat16 [7168], P('seq'), may hold values from -0.796875 to 0.796875
- embedding: bfloat16 [25600, 7168], P('mp', 'seq'), may hold values from -0.3984375 to 0.3984375
- score_weight: bfloat16 [7168], P('seq'), may hold values from -0.0625 to 0.0625
Outputs:
- hidden_states: bfloat16 [192, 7168], P(None, 'seq')
- score_values: float32 [96], replicated
- hidden_norms: float32 [192], replicated
- top_logits: float32 [96], replicated
Inputs may be any that keep to these rules, and one draw needn't show every extreme that they name: `prompt_lengths`: the longest prompt has exactly 8192 positions. `tail_lengths`: some continuation has exactly 256 tail tokens. `prompt_of`: each prompt is extended by 16 continuations or one more. `page_table`: all entries are distinct, so every pool page belongs to one continuation.
All inputs are finite; a program needn't handle non-finite values.
Results may differ from a plain program's by a relative error of at most 0.017.
The roundings to bfloat16 on the way count: a program that leaves them out, or rounds other values in their place, can miss the bound.
Values may be sent and summed in bfloat16 or wider, within the bound.
A program may use at most 128 MiB of HBM per device.

v0:
```python
import math
import jax
import jax.numpy as jnp
from jax import lax
from jax.sharding import PartitionSpec as P

D = 7168
HD = 128
PAGE = 128
epsilon = 1e-05
neg_fill = -1e30


def combine_parts(first, second):
    first_max, first_total, first_sum = first
    second_max, second_total, second_sum = second
    greatest = jnp.maximum(first_max, second_max)
    first_factor = jnp.exp(first_max - greatest)
    second_factor = jnp.exp(second_max - greatest)
    totals = first_total * first_factor + second_total * second_factor
    summed = first_sum * first_factor[..., None] + second_sum * second_factor[..., None]
    return (greatest, totals, summed)


def attend(queries, keys, values, valid, score_scale):
    scores = (
        jnp.einsum("cthe,nhe->chtn", queries, keys, preferred_element_type=jnp.float32)
        * score_scale
    )
    masked = valid[:, None, :, :]
    scores = jnp.where(masked, scores, neg_fill)
    greatest = jnp.max(scores, axis=-1)
    weights = jnp.where(masked, jnp.exp(scores - greatest[..., None]), 0.0)
    totals = jnp.sum(weights, axis=-1)
    summed = jnp.einsum(
        "chtn,nhe->chte", weights.astype(jnp.bfloat16), values, preferred_element_type=jnp.float32
    )
    return (greatest, totals, summed)


def per_device(
    token_ids,
    prompt_lengths,
    tail_lengths,
    prompt_of,
    page_table,
    prompt_keys,
    prompt_values,
    tail_keys,
    tail_values,
    norm_gain,
    norm_bias,
    qkv_weight,
    qkv_bias,
    out_weight,
    out_bias,
    embedding,
    score_weight,
):
    cont_count = token_ids.shape[0]
    row_count = 2 * cont_count
    vocab_local = embedding.shape[0]
    seq_index = lax.axis_index("seq")
    mp_index = lax.axis_index("mp")
    local_ids = token_ids.reshape(row_count) - mp_index * vocab_local
    inside = (local_ids >= 0) & (local_ids < vocab_local)
    picked = jnp.take(embedding, jnp.clip(local_ids, 0, vocab_local - 1), axis=0).astype(
        jnp.float32
    )
    picked = jnp.where(inside[:, None], picked, 0.0)
    inputs = lax.psum(picked, "mp").astype(jnp.bfloat16).astype(jnp.float32)
    input_sum, input_sq = lax.psum(
        (jnp.sum(inputs, axis=1), jnp.sum(inputs * inputs, axis=1)), "seq"
    )
    average = input_sum / D
    variance = input_sq / D - average * average
    gains = norm_gain.astype(jnp.float32)
    offsets = norm_bias.astype(jnp.float32)
    normed = (
        (inputs - average[:, None]) * lax.rsqrt(variance + epsilon)[:, None] * gains[0] + offsets[0]
    ).astype(jnp.bfloat16)
    partial_qkv = jnp.einsum("rd,dke->rke", normed, qkv_weight, preferred_element_type=jnp.float32)
    bias_rows = qkv_bias.astype(jnp.float32)
    qkv = (lax.psum(partial_qkv, "seq") + bias_rows).astype(jnp.bfloat16)
    head_local = qkv.shape[2] // HD
    queries = qkv[:, 0].reshape(cont_count, 2, head_local, HD)
    new_keys = qkv[:, 1].reshape(cont_count, 2, head_local, HD)
    new_values = qkv[:, 2].reshape(cont_count, 2, head_local, HD)
    score_scale = 1.0 / math.sqrt(HD)
    prompt_count = prompt_keys.shape[0]
    starts = jnp.cumsum(prompt_lengths) - prompt_lengths
    prompt_pick = (
        prompt_of[:, None] == jnp.arange(prompt_lengths.shape[0], dtype=jnp.int32)[None, :]
    ).astype(jnp.int32)
    begin = jnp.sum(prompt_pick * starts[None, :], axis=1)
    finish = begin + jnp.sum(prompt_pick * prompt_lengths[None, :], axis=1)
    position = seq_index * prompt_count + jnp.arange(prompt_count, dtype=jnp.int32)
    prompt_mask = (position[None, :] >= begin[:, None]) & (position[None, :] < finish[:, None])
    prompt_part = attend(
        queries,
        prompt_keys.reshape(prompt_count, head_local, HD),
        prompt_values.reshape(prompt_count, head_local, HD),
        prompt_mask[:, None, :],
        score_scale,
    )
    tail_count = tail_keys.shape[0]
    pages_local = tail_count // PAGE
    page_ids = seq_index * pages_local + jnp.arange(pages_local, dtype=jnp.int32)
    owned = page_table[:, :, None] == page_ids[None, None, :]
    offsets_tail = (
        jnp.arange(2, dtype=jnp.int32)[:, None] * PAGE + jnp.arange(PAGE, dtype=jnp.int32)[None, :]
    )
    filled = offsets_tail[None, :, :] < tail_lengths[:, None, None]
    tail_mask = jnp.any(owned[:, :, :, None] & filled[:, :, None, :], axis=1).reshape(
        cont_count, tail_count
    )
    tail_part = attend(
        queries,
        tail_keys.reshape(tail_count, head_local, HD),
        tail_values.reshape(tail_count, head_local, HD),
        tail_mask[:, None, :],
        score_scale,
    )
    local_part = combine_parts(prompt_part, tail_part)
    greatest = lax.pmax(local_part[0], "seq")
    factor = jnp.exp(local_part[0] - greatest)
    totals, summed = lax.psum((local_part[1] * factor, local_part[2] * factor[..., None]), "seq")
    merged = (greatest, totals, summed)
    self_scores = (
        jnp.einsum("cthe,cshe->chts", queries, new_keys, preferred_element_type=jnp.float32)
        * score_scale
    )
    causal = (jnp.arange(2, dtype=jnp.int32)[:, None] >= jnp.arange(2, dtype=jnp.int32)[None, :])[
        None, None, :, :
    ]
    self_scores = jnp.where(causal, self_scores, neg_fill)
    self_max = jnp.max(self_scores, axis=-1)
    self_weights = jnp.where(causal, jnp.exp(self_scores - self_max[..., None]), 0.0)
    self_total = jnp.sum(self_weights, axis=-1)
    self_sum = jnp.einsum(
        "chts,cshe->chte",
        self_weights.astype(jnp.bfloat16),
        new_values,
        preferred_element_type=jnp.float32,
    )
    greatest, totals, summed = combine_parts(merged, (self_max, self_total, self_sum))
    attended = (
        (summed / totals[..., None])
        .transpose(0, 2, 1, 3)
        .reshape(row_count, head_local * HD)
        .astype(jnp.bfloat16)
    )
    projected = jnp.dot(attended, out_weight, preferred_element_type=jnp.float32)
    hidden = inputs + lax.psum(projected, "mp") + out_bias.astype(jnp.float32)
    hidden_sum, hidden_sq = lax.psum(
        (jnp.sum(hidden, axis=1), jnp.sum(hidden * hidden, axis=1)), "seq"
    )
    hidden_norms = jnp.sqrt(hidden_sq / D)
    last_rows = hidden.reshape(cont_count, 2, hidden.shape[1])[:, 1]
    last_average = hidden_sum.reshape(cont_count, 2)[:, 1] / D
    last_variance = hidden_sq.reshape(cont_count, 2)[:, 1] / D - last_average * last_average
    final = (
        (last_rows - last_average[:, None]) * lax.rsqrt(last_variance + epsilon)[:, None] * gains[1]
        + offsets[1]
    ).astype(jnp.bfloat16)
    score_values = lax.psum(jnp.dot(final, score_weight, preferred_element_type=jnp.float32), "seq")
    logit_share = lax.psum_scatter(
        lax.dot_general(
            embedding, final, (((1,), (1,)), ((), ())), preferred_element_type=jnp.float32
        ),
        "seq",
        scatter_dimension=0,
        tiled=True,
    )
    top_logits = lax.pmax(jnp.max(logit_share, axis=0), ("seq", "mp"))
    return (hidden.astype(jnp.bfloat16), score_values, hidden_norms, top_logits)


def solution(mesh):
    return jax.shard_map(
        per_device,
        mesh=mesh,
        in_specs=(
            P(),
            P(),
            P(),
            P(),
            P(),
            P("seq", "mp"),
            P("seq", "mp"),
            P("seq", "mp"),
            P("seq", "mp"),
            P(None, "seq"),
            P(None, "seq"),
            P("seq", None, "mp"),
            P(None, "mp"),
            P("mp", "seq"),
            P("seq"),
            P("mp", "seq"),
            P("seq"),
        ),
        out_specs=(P(None, "seq"), P(), P(), P()),
        check_vma=False,
    )
```

profile of v0, /device:TPU:1, one launch (start us, length us, event | category | flops | bytes accessed | tf_op | source)
XLA Modules:
  0.0 1449.8 jit_solution(1172715131099909362)
XLA Ops:
  9.1 1.5 copy.159
  11.8 30.5 %psum.70 = bf16[192,112]{1,0:T(8,128)(2,1)S(1)} all-reduce(f32[192,112]{1,0:T(8,128)S(1)} %convert_select_fusion), channel_id=1, replica_groups=mesh['seq'=64,'mp'=8] {'mp'}, use_global_device_ids=true, to_apply=%region_0.1 | all-reduce | flops 21504 | bytes 129024 | tf_op jit(solution)/shard_map/psum | solution.py:71
  43.1 131.9 %all-reduce.2 = (f32[192]{0:T(256)S(1)}, f32[192]{0:T(256)S(1)}) all-reduce(f32[192]{0:T(256)S(1)} %get-tuple-element.9, f32[192]{0:T(256)S(1)} %get-tuple-element.8), channel_id=1, replica_groups=mesh['seq'=64,'mp'=8] {'seq'}, use_global_device_ids=true, to_apply=%region_7.8 | all-reduce | flops 384 | bytes 3072 | tf_op jit(solution)/shard_map/psum | solution.py:72
  175.0 1.7 fusion.51
  178.8 2.4 copy.163
  183.5 178.7 %all-reduce.8.cloned.1.call-done = f32[192,3,768]{2,0,1:T(8,128)} async-done(((f32[192,3,768]{2,0,1:T(8,128)}), f32[192,3,768]{2,0,1:T(8,128)}) %all-reduce.8.cloned.1.call-update) | async-done | bytes 1769488 | tf_op jit(solution)/shard_map/psum | solution.py:84
  362.2 1.6 add_convert_fusion
  367.1 1.8 bitcast_reduce_fusion.1
  368.9 1.3 fusion.16
  372.9 1.8 fusion.2
  374.7 128.4 %pmax.14 = f32[96,6,2]{0,2,1:T(2,128)} all-reduce(f32[96,6,2]{0,2,1:T(2,128)} %max.21), channel_id=1, replica_groups=mesh['seq'=64,'mp'=8] {'seq'}, use_global_device_ids=true, to_apply=%region_12.13 | all-reduce | flops 1152 | bytes 9216 | tf_op jit(solution)/shard_map/pmax | solution.py:125
  503.0 1.4 add_multiply_fusion
  504.4 130.1 %psum.75 = f32[96,6,2]{0,2,1:T(2,128)} all-reduce(f32[96,6,2]{0,2,1:T(2,128)} %get-tuple-element.22), channel_id=1, replica_groups=mesh['seq'=64,'mp'=8] {'seq'}, use_global_device_ids=true, to_apply=%region_17.18 | all-reduce | flops 1152 | bytes 9216 | tf_op jit(solution)/shard_map/psum | solution.py:127
  634.5 3.3 fusion.18
  638.0 1.7 fusion.15
  641.4 184.1 %all-reduce.10.cloned.1.call-done = f32[96,6,2,128]{3,0,2,1:T(8,128)} async-done(((f32[96,6,2,128]{3,0,2,1:T(8,128)}), f32[96,6,2,128]{3,0,2,1:T(8,128)}) %all-reduce.10.cloned.1.call-update) | async-done | bytes 589840 | tf_op jit(solution)/shard_map/psum | solution.py:127
  825.5 1.7 fusion.34
  828.4 74.0 %all-reduce.12.cloned.1.call-done = f32[192,112]{1,0:T(8,128)} async-done(((f32[192,112]{1,0:T(8,128)}), f32[192,112]{1,0:T(8,128)}) %all-reduce.12.cloned.1.call-update) | async-done | bytes 86032 | tf_op jit(solution)/shard_map/psum | solution.py:154
  903.6 245.9 %all-reduce.1 = (f32[96,2]{1,0:T(8,128)S(1)}, f32[192]{0:T(256)S(1)}) all-reduce(f32[96,2]{1,0:T(8,128)S(1)} %reshape.242, f32[192]{0:T(256)S(1)} %get-tuple-element.5), channel_id=1, replica_groups=mesh['seq'=64,'mp'=8] {'seq'}, use_global_device_ids=true, to_apply=%region_21.22 | all-reduce | flops 384 | bytes 3072 | tf_op jit(solution)/shard_map/psum | solution.py:155
  1150.0 1.4 convolution_bitcast_fusion
  1151.4 1.3 dynamic-slice
  1154.1 129.6 %psum.79 = f32[96]{0:T(128)} all-reduce(f32[96]{0:T(128)S(1)} %convolution_bitcast_fusion.2), channel_id=1, replica_groups=mesh['seq'=64,'mp'=8] {'seq'}, use_global_device_ids=true, to_apply=%region_24.25 | all-reduce | flops 96 | bytes 768 | tf_op jit(solution)/shard_map/psum | solution.py:166
  1284.3 58.6 %all-reduce.14.cloned.1.call-done = f32[3200,96]{0,1:T(8,128)} async-done(((f32[3200,96]{0,1:T(8,128)}), f32[3200,96]{0,1:T(8,128)}) %all-reduce.14.cloned.1.call-update) | async-done | bytes 1228816
  1343.9 99.3 %pmax.15 = f32[96]{0:T(128)} all-reduce(f32[96]{0:T(128)S(1)} %dynamic-slice_reduce_fusion), channel_id=1, replica_groups=mesh['seq'=64,'mp'=8] {'seq','mp'}, use_global_device_ids=true, to_apply=%region_27.28 | all-reduce | flops 96 | bytes 768 | tf_op jit(solution)/shard_map/pmax | solution.py:175
  (140 shorter events, 20.9 us)
Async XLA Ops:
  7.2 167.8 %copy-start = (bf16[112,3,768]{2,0,1:T(8,128)(2,1)S(1)}, bf16[112,3,768]{2,0,1:T(8,128)(2,1)}, u32[]{:S(2)}) copy-start(bf16[112,3,768]{2,0,1:T(8,128)(2,1)} %param.28) | copy-start | bytes 1548292
  7.2 35.1 %copy-start.32 = (bf16[2,112]{1,0:T(2,128)(2,1)S(1)}, bf16[2,112]{1,0:T(2,128)(2,1)}, u32[]{:S(2)}) copy-start(bf16[2,112]{1,0:T(2,128)(2,1)} %param.27) | copy-start | bytes 1348
  7.2 35.2 %copy-start.33 = (bf16[2,112]{1,0:T(2,128)(2,1)S(1)}, bf16[2,112]{1,0:T(2,128)(2,1)}, u32[]{:S(2)}) copy-start(bf16[2,112]{1,0:T(2,128)(2,1)} %param.26) | copy-start | bytes 1348
  7.2 355.0 %all-reduce.8.cloned.1.call-start = ((), (), s32[]{:S(2)}) async-start(), calls=%async_computation | async-start | bytes 3538944 | tf_op jit(solution)/shard_map/psum | solution.py:84
  42.3 134.4 %copy-start.8 = (bf16[192,112]{1,0:T(8,128)(2,1)}, bf16[192,112]{1,0:T(8,128)(2,1)S(1)}, u32[]{:S(2)}) copy-start(bf16[192,112]{1,0:T(8,128)(2,1)S(1)} %psum.70) | copy-start | bytes 129028
  176.7 648.8 %all-reduce.10.cloned.1.call-start = ((), (), s32[]{:S(2)}) async-start(), calls=%async_computation.1 | async-start | bytes 1179648 | tf_op jit(solution)/shard_map/psum | solution.py:127
  178.2 3.1 copy-start.11
  178.8 3.5 copy-start.27
  178.8 3.6 copy-start.29
  178.8 3.7 copy-start.30
  372.9 261.7 %copy-start.6 = (bf16[768,768]{0,1:T(8,128)(2,1)S(1)}, bf16[768,768]{0,1:T(8,128)(2,1)}, u32[]{:S(2)}) copy-start(bf16[768,768]{0,1:T(8,128)(2,1)} %copy.163) | copy-start | bytes 3538948
  634.5 3.3 copy-start.12
  634.5 3.3 copy-start.14
  634.5 3.3 copy-start.23
  634.5 3.4 copy-start.24
  639.6 262.7 %all-reduce.12.cloned.1.call-start = ((), (), s32[]{:S(2)}) async-start(), calls=%async_computation.2 | async-start | bytes 196608 | tf_op jit(solution)/shard_map/psum | solution.py:154
  640.6 186.8 %copy-start.15 = (bf16[768,112]{0,1:T(8,128)(2,1)S(1)}, bf16[768,112]{0,1:T(8,128)(2,1)}, u32[]{:S(2)}) copy-start(bf16[768,112]{0,1:T(8,128)(2,1)} %param.30) | copy-start | bytes 516100
  641.3 187.0 %copy-start.34 = (bf16[112]{0:T(256)(128)(2,1)S(1)}, bf16[112]{0:T(256)(128)(2,1)}, u32[]{:S(2)}) copy-start(bf16[112]{0:T(256)(128)(2,1)} %param.31) | copy-start | bytes 676
  641.3 261.0 %copy-start.9 = (bf16[192,112]{1,0:T(8,128)(2,1)S(1)}, bf16[192,112]{1,0:T(8,128)(2,1)}, u32[]{:S(2)}) copy-start(bf16[192,112]{1,0:T(8,128)(2,1)} %copy-done.8) | copy-start | bytes 129028
  641.4 508.5 %copy-start.25 = (f32[112]{0:T(128)S(1)}, f32[112]{0:T(128)}, u32[]{:S(2)}) copy-start(f32[112]{0:T(128)} %get-tuple-element.31) | copy-start | bytes 1348
  641.4 508.5 %copy-start.26 = (f32[112]{0:T(128)S(1)}, f32[112]{0:T(128)}, u32[]{:S(2)}) copy-start(f32[112]{0:T(128)} %get-tuple-element.40) | copy-start | bytes 1348
  825.5 324.5 %copy-start.2 = (bf16[3200,112]{0,1:T(8,128)(2,1)S(1)}, bf16[3200,112]{0,1:T(8,128)(2,1)}, u32[]{:S(2)}) copy-start(bf16[3200,112]{0,1:T(8,128)(2,1)} %param.32) | copy-start | bytes 2150404
  828.3 514.5 %all-reduce.14.cloned.1.call-start = ((), (), s32[]{:S(2)}) async-start(), calls=%async_computation.3 | async-start | bytes 2457600
  1149.7 4.3 copy-start.31
  (15 other events, 28.7 us)
Sparse Core Ops, SparseCore 0:
  176.8 185.3 all-reduce.7
  639.8 185.7 all-reduce.9
  828.4 73.9 all-reduce.11
  1151.5 191.2 all-reduce.13
where the time goes:
time: 1450 us
  blocking collectives  896 us (62%)
  waiting for transfers between devices  495 us (34%)
  other arithmetic  15.3 us (1%)
  between operations  15 us (1%)
  local copies, waits for them, and re-layouts  14.7 us (1%)
    psum x1, blocking collectives, per_device(): lax.psum((jnp.sum(hidden, axis=1), jnp.sum(hidden * hidden, axis=1)), 'seq')  246 us
    psum x1, waiting for transfers between devices, per_device(): lax.psum((local_part[1] * factor, local_part[2] * factor[..., None]), 'seq')  184 us
    psum x1, waiting for transfers between devices, per_device(): qkv = (lax.psum(partial_qkv, 'seq') + bias_rows).astype(jnp.bfloat16)  179 us
    psum x1, blocking collectives, per_device(): lax.psum((jnp.sum(inputs, axis=1), jnp.sum(inputs * inputs, axis=1)), 'seq')  132 us
    psum x1, blocking collectives, per_device(): lax.psum((local_part[1] * factor, local_part[2] * factor[..., None]), 'seq')  130 us
    psum x1, blocking collectives, per_device(): lax.psum(jnp.dot(final, score_weight, preferred_element_type=jnp.float32)...  130 us
    pmax x1, blocking collectives, per_device(): greatest = lax.pmax(local_part[0], 'seq')  128 us
    pmax x1, blocking collectives, per_device(): top_logits = lax.pmax(jnp.max(logit_share, axis=0), ('seq', 'mp'))  99.3 us
  transfers between devices with their start and end apart: 4, of which 4 were waited for; matrix products, arithmetic and copies ran while one was open for 1% of the time, Pallas kernels for 0%

commit v1 on v0

--- a/solution.py
+++ b/solution.py
@@ -163,7 +163,10 @@
         (last_rows - last_average[:, None]) * lax.rsqrt(last_variance + epsilon)[:, None] * gains[1]
         + offsets[1]
     ).astype(jnp.bfloat16)
-    score_values = lax.psum(jnp.dot(final, score_weight, preferred_element_type=jnp.float32), "seq")
+    score_values = jnp.sum(
+        lax.all_gather(jnp.dot(final, score_weight, preferred_element_type=jnp.float32), "seq"),
+        axis=0,
+    )
     logit_share = lax.psum_scatter(
         lax.dot_general(
             embedding, final, (((1,), (1,)), ((), ())), preferred_element_type=jnp.float32

time: 1450 us -> 1510 us (1.041)
  blocking collectives: 896 us -> 1010 us
  waiting for transfers between devices: 495 us -> 437 us
    unnamed x0 -> x1, blocking collectives: none -> 246 us
    psum x1 -> x0, blocking collectives: 130 us -> none  [per_device(): lax.psum(jnp.dot(final, score_weight, preferred_element_type=jnp.float32)...]
    unnamed x5, waiting for transfers between devices: 58.6 us -> 0.07 us
  transfers between devices with their start and end apart: 4 -> 4, of which waited for: 4 -> 3; matrix products, arithmetic and copies ran while one was open for 1% -> 1% of each run, Pallas kernels for 0% -> 0%
where the time goes in v1:
time: 1510 us
  blocking collectives  1010 us (67%)
  waiting for transfers between devices  437 us (29%)
  other arithmetic  15.9 us (1%)
  between operations  15.7 us (1%)
    unnamed x1, blocking collectives  246 us
    psum x1, blocking collectives, per_device(): lax.psum((jnp.sum(hidden, axis=1), jnp.sum(hidden * hidden, axis=1)), 'seq')  246 us
    psum x1, waiting for transfers between devices, per_device(): lax.psum((local_part[1] * factor, local_part[2] * factor[..., None]), 'seq')  184 us
    psum x1, waiting for transfers between devices, per_device(): qkv = (lax.psum(partial_qkv, 'seq') + bias_rows).astype(jnp.bfloat16)  179 us
    psum x1, blocking collectives, per_device(): lax.psum((jnp.sum(inputs, axis=1), jnp.sum(inputs * inputs, axis=1)), 'seq')  132 us
    psum x1, blocking collectives, per_device(): lax.psum((local_part[1] * factor, local_part[2] * factor[..., None]), 'seq')  130 us
    pmax x1, blocking collectives, per_device(): greatest = lax.pmax(local_part[0], 'seq')  128 us
    pmax x1, blocking collectives, per_device(): top_logits = lax.pmax(jnp.max(logit_share, axis=0), ('seq', 'mp'))  97.9 us
  transfers between devices with their start and end apart: 4, of which 3 were waited for; matrix products, arithmetic and copies ran while one was open for 1% of the time, Pallas kernels for 0%

profile of v1, /device:TPU:1, one launch (start us, length us, event | category | flops | bytes accessed | tf_op | source)
XLA Modules:
  0.0 1507.3 jit_solution(12532436178633487252)
XLA Ops:
  9.1 1.5 copy.159
  11.8 30.5 %psum.63 = bf16[192,112]{1,0:T(8,128)(2,1)S(1)} all-reduce(f32[192,112]{1,0:T(8,128)S(1)} %convert_select_fusion), channel_id=1, replica_groups=mesh['seq'=64,'mp'=8] {'mp'}, use_global_device_ids=true, to_apply=%region_0.1 | all-reduce | flops 21504 | bytes 129024 | tf_op jit(solution)/shard_map/psum | solution.py:71
  43.1 131.9 %all-reduce.3 = (f32[192]{0:T(256)S(1)}, f32[192]{0:T(256)S(1)}) all-reduce(f32[192]{0:T(256)S(1)} %get-tuple-element.9, f32[192]{0:T(256)S(1)} %get-tuple-element.8), channel_id=1, replica_groups=mesh['seq'=64,'mp'=8] {'seq'}, use_global_device_ids=true, to_apply=%region_7.8 | all-reduce | flops 384 | bytes 3072 | tf_op jit(solution)/shard_map/psum | solution.py:72
  175.0 1.7 fusion.51
  178.8 2.4 copy.163
  181.2 1.1 copy.169
  183.5 178.7 %all-reduce.9.cloned.1.call-done = f32[192,3,768]{2,0,1:T(8,128)} async-done(((f32[192,3,768]{2,0,1:T(8,128)}), f32[192,3,768]{2,0,1:T(8,128)}) %all-reduce.9.cloned.1.call-update) | async-done | bytes 1769488 | tf_op jit(solution)/shard_map/psum | solution.py:84
  362.2 1.6 add_convert_fusion
  367.1 1.8 bitcast_reduce_fusion.1
  368.9 1.3 fusion.16
  371.7 1.1 copy-done.1
  372.9 1.8 fusion.2
  374.7 128.4 %pmax.14 = f32[96,6,2]{0,2,1:T(2,128)} all-reduce(f32[96,6,2]{0,2,1:T(2,128)} %max.21), channel_id=1, replica_groups=mesh['seq'=64,'mp'=8] {'seq'}, use_global_device_ids=true, to_apply=%region_12.13 | all-reduce | flops 1152 | bytes 9216 | tf_op jit(solution)/shard_map/pmax | solution.py:125
  503.0 1.4 add_multiply_fusion
  504.4 130.1 %psum.68 = f32[96,6,2]{0,2,1:T(2,128)} all-reduce(f32[96,6,2]{0,2,1:T(2,128)} %get-tuple-element.22), channel_id=1, replica_groups=mesh['seq'=64,'mp'=8] {'seq'}, use_global_device_ids=true, to_apply=%region_17.18 | all-reduce | flops 1152 | bytes 9216 | tf_op jit(solution)/shard_map/psum | solution.py:127
  634.5 3.3 fusion.18
  638.0 1.7 fusion.15
  641.4 184.1 %all-reduce.11.cloned.1.call-done = f32[96,6,2,128]{3,0,2,1:T(8,128)} async-done(((f32[96,6,2,128]{3,0,2,1:T(8,128)}), f32[96,6,2,128]{3,0,2,1:T(8,128)}) %all-reduce.11.cloned.1.call-update) | async-done | bytes 589840 | tf_op jit(solution)/shard_map/psum | solution.py:127
  825.5 1.7 fusion.34
  828.4 74.0 %all-reduce.13.cloned.1.call-done = f32[192,112]{1,0:T(8,128)} async-done(((f32[192,112]{1,0:T(8,128)}), f32[192,112]{1,0:T(8,128)}) %all-reduce.13.cloned.1.call-update) | async-done | bytes 86032 | tf_op jit(solution)/shard_map/psum | solution.py:154
  903.6 245.9 %all-reduce.2 = (f32[96,2]{1,0:T(8,128)S(1)}, f32[192]{0:T(256)S(1)}) all-reduce(f32[96,2]{1,0:T(8,128)S(1)} %reshape.242, f32[192]{0:T(256)S(1)} %get-tuple-element.5), channel_id=1, replica_groups=mesh['seq'=64,'mp'=8] {'seq'}, use_global_device_ids=true, to_apply=%region_21.22 | all-reduce | flops 384 | bytes 3072 | tf_op jit(solution)/shard_map/psum | solution.py:155
  1150.0 1.4 convolution_bitcast_fusion
  1154.3 246.3 %all-reduce = f32[6144]{0:T(1024)S(1)} all-reduce(f32[6144]{0:T(1024)S(1)} %dynamic-update-slice), channel_id=2, replica_groups=mesh['seq'=64,'mp'=8] {'seq'}, use_global_device_ids=true, to_apply=%add | all-reduce | flops 6144 | bytes 49152
  1402.8 97.9 %pmax.15 = f32[96]{0:T(128)} all-reduce(f32[96]{0:T(128)S(1)} %dynamic-slice_reduce_fusion), channel_id=1, replica_groups=mesh['seq'=64,'mp'=8] {'seq','mp'}, use_global_device_ids=true, to_apply=%region_27.28 | all-reduce | flops 96 | bytes 768 | tf_op jit(solution)/shard_map/pmax | solution.py:178
  (146 shorter events, 20.1 us)
Async XLA Ops:
  7.2 167.8 %copy-start = (bf16[112,3,768]{2,0,1:T(8,128)(2,1)S(1)}, bf16[112,3,768]{2,0,1:T(8,128)(2,1)}, u32[]{:S(2)}) copy-start(bf16[112,3,768]{2,0,1:T(8,128)(2,1)} %param.28) | copy-start | bytes 1548292
  7.2 35.1 %copy-start.33 = (bf16[2,112]{1,0:T(2,128)(2,1)S(1)}, bf16[2,112]{1,0:T(2,128)(2,1)}, u32[]{:S(2)}) copy-start(bf16[2,112]{1,0:T(2,128)(2,1)} %param.27) | copy-start | bytes 1348
  7.2 35.2 %copy-start.34 = (bf16[2,112]{1,0:T(2,128)(2,1)S(1)}, bf16[2,112]{1,0:T(2,128)(2,1)}, u32[]{:S(2)}) copy-start(bf16[2,112]{1,0:T(2,128)(2,1)} %param.26) | copy-start | bytes 1348
  7.2 355.0 %all-reduce.9.cloned.1.call-start = ((), (), s32[]{:S(2)}) async-start(), calls=%async_computation | async-start | bytes 3538944 | tf_op jit(solution)/shard_map/psum | solution.py:84
  42.3 134.4 %copy-start.8 = (bf16[192,112]{1,0:T(8,128)(2,1)}, bf16[192,112]{1,0:T(8,128)(2,1)S(1)}, u32[]{:S(2)}) copy-start(bf16[192,112]{1,0:T(8,128)(2,1)S(1)} %psum.63) | copy-start | bytes 129028
  176.7 648.8 %all-reduce.11.cloned.1.call-start = ((), (), s32[]{:S(2)}) async-start(), calls=%async_computation.1 | async-start | bytes 1179648 | tf_op jit(solution)/shard_map/psum | solution.py:127
  178.8 3.5 copy-start.27
  178.8 3.6 copy-start.30
  178.8 3.7 copy-start.31
  372.9 261.7 %copy-start.6 = (bf16[768,768]{0,1:T(8,128)(2,1)S(1)}, bf16[768,768]{0,1:T(8,128)(2,1)}, u32[]{:S(2)}) copy-start(bf16[768,768]{0,1:T(8,128)(2,1)} %copy.163) | copy-start | bytes 3538948
  634.5 3.3 copy-start.12
  634.5 3.3 copy-start.14
  634.5 3.3 copy-start.23
  634.5 3.4 copy-start.24
  639.6 262.7 %all-reduce.13.cloned.1.call-start = ((), (), s32[]{:S(2)}) async-start(), calls=%async_computation.2 | async-start | bytes 196608 | tf_op jit(solution)/shard_map/psum | solution.py:154
  640.6 186.8 %copy-start.15 = (bf16[768,112]{0,1:T(8,128)(2,1)S(1)}, bf16[768,112]{0,1:T(8,128)(2,1)}, u32[]{:S(2)}) copy-start(bf16[768,112]{0,1:T(8,128)(2,1)} %param.30) | copy-start | bytes 516100
  641.3 187.0 %copy-start.35 = (bf16[112]{0:T(256)(128)(2,1)S(1)}, bf16[112]{0:T(256)(128)(2,1)}, u32[]{:S(2)}) copy-start(bf16[112]{0:T(256)(128)(2,1)} %param.31) | copy-start | bytes 676
  641.3 261.0 %copy-start.9 = (bf16[192,112]{1,0:T(8,128)(2,1)S(1)}, bf16[192,112]{1,0:T(8,128)(2,1)}, u32[]{:S(2)}) copy-start(bf16[192,112]{1,0:T(8,128)(2,1)} %copy-done.8) | copy-start | bytes 129028
  641.4 508.5 %copy-start.25 = (f32[112]{0:T(128)S(1)}, f32[112]{0:T(128)}, u32[]{:S(2)}) copy-start(f32[112]{0:T(128)} %get-tuple-element.33) | copy-start | bytes 1348
  641.4 508.5 %copy-start.26 = (f32[112]{0:T(128)S(1)}, f32[112]{0:T(128)}, u32[]{:S(2)}) copy-start(f32[112]{0:T(128)} %get-tuple-element.42) | copy-start | bytes 1348
  825.5 324.5 %copy-start.2 = (bf16[3200,112]{0,1:T(8,128)(2,1)S(1)}, bf16[3200,112]{0,1:T(8,128)(2,1)}, u32[]{:S(2)}) copy-start(bf16[3200,112]{0,1:T(8,128)(2,1)} %param.32) | copy-start | bytes 2150404
  828.3 573.5 %all-reduce.15.cloned.1.call-start = ((), (), s32[]{:S(2)}) async-start(), calls=%async_computation.3 | async-start | bytes 2457600
  903.6 247.8 %copy-start.28 = (u32[512]{0:T(512)S(1)}, u32[512]{0:T(512)}, u32[]{:S(2)}) copy-start(u32[512]{0:T(512)} %constant.73) | copy-start | bytes 6148
  1149.7 4.3 copy-start.32
  (16 other events, 31.8 us)
Sparse Core Ops, SparseCore 0:
  176.8 185.3 all-reduce.8
  639.8 185.7 all-reduce.10
  828.4 73.9 all-reduce.12
  1151.5 191.1 all-reduce.14
